TPU v7x, 256 devices: a whole 4x4x8 slice. The times are simulated.
256 devices in a mesh: prefix: 32 (over z, y_lo, core), branch: 8 (over y_hi, x).
Axes of the slice: x: 4, y: 4 (y_hi: 2, y_lo: 2; y = y_hi * 2 + y_lo), z: 8, core: 2. Of those that a mesh axis runs over, the one named last changes fastest.
Arguments:
- queries: bfloat16 [32, 8, 256, 4096], P('prefix', 'branch'), may hold values from -5 to 5
- branch_kv: bfloat16 [32, 8, 2, 256, 512], P('prefix', 'branch'), may hold values from -5 to 5
- prefix_kv: bfloat16 [32, 2, 512, 512], P('prefix', None, 'branch'), may hold values from -6 to 6
- out_grad: bfloat16 [32, 8, 256, 4096], P('prefix', 'branch'), may hold values from -6 to 6
- value_weight: float32 [4096], replicated, may hold values from -1.5 to 1.5
- value_grad: float32 [32, 8, 256], P('prefix', 'branch'), may hold values from -6 to 6
- parents: int32 [32], replicated, may hold values from 0 to 31
- lengths: int32 [32, 8], P('prefix', 'branch'), may hold values from 128 to 256, as said below
Outputs:
- values: float32 [32, 8, 256], P('prefix', 'branch')
- query_grad: bfloat16 [32, 8, 256, 4096], P('prefix', 'branch')
- branch_kv_grad: bfloat16 [32, 8, 2, 256, 512], P('prefix', 'branch')
- prefix_kv_grad: float32 [32, 2, 512, 512], P('prefix', None, 'branch')
Inputs may be any that keep to these rules, and one draw needn't show every extreme that they name: `lengths`: each length is a multiple of 128; some branch has 256.
All inputs are finite; a program needn't handle non-finite values.
Results may differ from a plain program's by a relative error of at most 0.0092.
Values may be sent and summed in bfloat16 or wider, within the bound.
No kernel may reach another device: no remote copies, remote signals or barrier semaphores. Data moves between devices by JAX's collectives and lax.ppermute only.
A program may use at most 64 MiB of HBM per device.

v0:
```python
import jax
import jax.numpy as jnp
from jax import lax
from jax.sharding import PartitionSpec as P

QH = 32
KVH = 4
HD = 128


NEG_FILL = -1e30


def shards(queries, branch_kv, prefix_kv, out_grad, value_weight, value_grad, parents, lengths):
    owner = lax.axis_index("prefix")
    my_parent = lax.dynamic_slice_in_dim(parents, owner, 1, 0)[0]
    score_scale = HD ** (-0.5)
    head_ratio = QH // KVH
    head_width = head_ratio * HD
    gathered = lax.all_gather(prefix_kv, "prefix", axis=0, tiled=True)
    picked = lax.dynamic_slice_in_dim(gathered, my_parent, 1, 0)
    whole_prefix = lax.all_gather(picked, "branch", axis=2, tiled=True)
    prefix_len = whole_prefix.shape[2]
    key_rows = jnp.concatenate([whole_prefix[0, 0], branch_kv[0, 0, 0]], axis=0)
    value_rows = jnp.concatenate([whole_prefix[0, 1], branch_kv[0, 0, 1]], axis=0)
    query_block = queries[0, 0]
    query_len = query_block.shape[0]
    key_count = key_rows.shape[0]
    row_index = lax.broadcasted_iota(jnp.int32, (query_len, key_count), 0)
    col_index = lax.broadcasted_iota(jnp.int32, (query_len, key_count), 1)
    allowed = (col_index < prefix_len) | (col_index - prefix_len <= row_index)
    live_rows = lax.broadcasted_iota(jnp.int32, (query_len, 1), 0) < lengths[0, 0]
    out_cot = (
        out_grad[0, 0].astype(jnp.float32) + value_grad[0, 0][:, None] * value_weight[None, :]
    ).astype(jnp.bfloat16)

    def per_head(head_index, running):
        value_acc, query_acc, pair_acc = running
        query_part = lax.dynamic_slice_in_dim(query_block, head_index * head_width, head_width, 1)
        query_part = query_part.reshape(query_len, head_ratio, HD)
        cot_part = lax.dynamic_slice_in_dim(out_cot, head_index * head_width, head_width, 1)
        cot_part = cot_part.reshape(query_len, head_ratio, HD)
        key_part = lax.dynamic_slice_in_dim(key_rows, head_index * HD, HD, 1)
        value_part = lax.dynamic_slice_in_dim(value_rows, head_index * HD, HD, 1)
        weight_part = lax.dynamic_slice_in_dim(value_weight, head_index * head_width, head_width, 0)
        weight_part = weight_part.reshape(head_ratio, HD)
        scores = (
            jnp.einsum("trd,sd->rts", query_part, key_part, preferred_element_type=jnp.float32)
            * score_scale
        )
        scores = jnp.where(allowed[None], scores, NEG_FILL)
        row_max = jnp.max(scores, axis=2, keepdims=True)
        shifted = jnp.exp(scores - row_max)
        weights = shifted / jnp.sum(shifted, axis=2, keepdims=True)
        weights = jnp.where(live_rows[None], weights, 0.0)
        weights_low = weights.astype(jnp.bfloat16)
        attended = jnp.einsum(
            "rts,sd->trd", weights_low, value_part, preferred_element_type=jnp.float32
        )
        value_acc = value_acc + jnp.sum(attended * weight_part[None], axis=(1, 2))
        value_piece = jnp.einsum(
            "rts,trd->sd", weights_low, cot_part, preferred_element_type=jnp.float32
        )
        prob_grad = jnp.einsum(
            "trd,sd->rts", cot_part, value_part, preferred_element_type=jnp.float32
        )
        row_delta = jnp.transpose(jnp.sum(cot_part.astype(jnp.float32) * attended, axis=2))
        score_low = (weights * (prob_grad - row_delta[:, :, None])).astype(jnp.bfloat16)
        query_piece = (
            jnp.einsum("rts,sd->trd", score_low, key_part, preferred_element_type=jnp.float32)
            * score_scale
        )
        key_piece = (
            jnp.einsum("rts,trd->sd", score_low, query_part, preferred_element_type=jnp.float32)
            * score_scale
        )
        query_acc = lax.dynamic_update_slice_in_dim(
            query_acc,
            query_piece.astype(jnp.bfloat16).reshape(query_len, head_width),
            head_index * head_width,
            1,
        )
        pair_acc = lax.dynamic_update_slice_in_dim(
            pair_acc, jnp.stack([key_piece, value_piece]), head_index * HD, 2
        )
        return (value_acc, query_acc, pair_acc)

    start_state = (
        jnp.zeros((query_len,), jnp.float32),
        jnp.zeros((query_len, QH * HD), jnp.bfloat16),
        jnp.zeros((2, key_count, KVH * HD), jnp.float32),
    )
    value_acc, query_acc, pair_acc = lax.fori_loop(0, KVH, per_head, start_state)
    branch_grad = pair_acc[:, prefix_len:].astype(jnp.bfloat16)
    token_share = lax.psum_scatter(
        pair_acc[:, :prefix_len], "branch", scatter_dimension=1, tiled=True
    )
    targets = lax.broadcasted_iota(jnp.int32, (lax.axis_size("prefix") * 1, 1, 1, 1), 0)
    prefix_grad = lax.psum_scatter(
        jnp.where(targets == my_parent, token_share[None], 0.0),
        "prefix",
        scatter_dimension=0,
        tiled=True,
    )
    return (value_acc[None, None], query_acc[None, None], branch_grad[None, None], prefix_grad)


def solution(mesh):
    in_specs = (
        P("prefix", "branch", None, None),
        P("prefix", "branch", None, None, None),
        P("prefix", None, "branch", None),
        P("prefix", "branch", None, None),
        P(),
        P("prefix", "branch", None),
        P(),
        P("prefix", "branch"),
    )
    out_specs = (
        P("prefix", "branch", None),
        P("prefix", "branch", None, None),
        P("prefix", "branch", None, None, None),
        P("prefix", None, "branch", None),
    )
    return jax.shard_map(shards, mesh=mesh, in_specs=in_specs, out_specs=out_specs, check_vma=False)
```

profile of v0, /device:TPU:4, one launch (start us, length us, event | category | flops | bytes accessed | tf_op | source)
XLA Modules:
  0.0 441.0 jit_solution(4446570069672298126)
XLA Ops:
  11.1 68.5 %all-gather.3.cloned.1.call-done = bf16[32,2,64,512]{3,2,1,0:T(8,128)(2,1)} async-done(((bf16[1,2,64,512]{3,2,1,0:T(8,128)(2,1)}), bf16[32,2,64,512]{3,2,1,0:T(8,128)(2,1)}) %all-gather.3.cloned.1.call-update) | async-done | bytes 4194320 | tf_op jit(solution)/shard_map/all_gather | solution.py:20
  79.7 1.6 constant_dynamic-slice_fusion.2
  81.3 4.1 copy.42
  85.4 2.5 copy.41
  88.0 1.9 fusion.44
  89.9 43.5 %all-gather.5.cloned.1.call-done = bf16[1,2,512,512]{3,2,1,0:T(8,128)(2,1)} async-done(((bf16[1,2,64,512]{3,2,1,0:T(8,128)(2,1)}), bf16[1,2,512,512]{3,2,1,0:T(8,128)(2,1)}) %all-gather.5.cloned.1.call-update) | async-done | bytes 1048592 | tf_op jit(solution)/shard_map/all_gather | solution.py:22
  136.0 2.1 broadcast_in_dim.109
  138.1 1.6 broadcast_in_dim.108.clone
  139.7 75.8 %while.18 = (s32[]{:T(128)}, f32[256]{0:T(256)S(1)}, bf16[256,4096]{1,0:T(8,128)(2,1)}, f32[2,768,512]{2,1,0:T(8,128)}, bf16[768,512]{1,0:T(8,128)(2,1)}, /*inde...) while((s32[]{:T(128)}, f32[256]{0:T(256)S(1)}, ...), condition=%wide.region_5.6_spmd.clone, body=%wide.region_0.5_spmd.clone.sunk | while | flops 2437315840 | bytes 70186104 | solution.py:93
  141.0 5.7 %fusion.93 = (f32[8,256]{1,0:T(8,128)S(1)}, f32[8,256,768]{1,2,0:T(8,128)}) fusion(pred[256,768]{0,1:T(8,128)(4,1)S(1)} %fusion.92, bf16[256,8,128]{0,2,1:T(8,128)(2,1)S(1)} %bitcast.148, bf16[768,512]{1,0:T(8,128)(2,1)} %get-tuple-element.434, s32[]{:T(128)S(6)} %select_n.77), kind=kOutput, calls=%fused_computation.66.clone.1 | convolution fusion | flops 408945408 | bytes 7217156 | tf_op jit(solution)/shard_map/while/body/eval_jaxpr/sub | solution.py:53
  147.5 3.6 fusion.94
  159.9 5.7 %fusion.93 = (f32[8,256]{1,0:T(8,128)S(1)}, f32[8,256,768]{1,2,0:T(8,128)}) fusion(pred[256,768]{0,1:T(8,128)(4,1)S(1)} %fusion.92, bf16[256,8,128]{0,2,1:T(8,128)(2,1)S(1)} %bitcast.148, bf16[768,512]{1,0:T(8,128)(2,1)} %get-tuple-element.434, s32[]{:T(128)S(6)} %select_n.77), kind=kOutput, calls=%fused_computation.66.clone.1 | convolution fusion | flops 408945408 | bytes 7217156 | tf_op jit(solution)/shard_map/while/body/eval_jaxpr/sub | solution.py:53
  166.3 3.6 fusion.94
  178.8 5.7 %fusion.93 = (f32[8,256]{1,0:T(8,128)S(1)}, f32[8,256,768]{1,2,0:T(8,128)}) fusion(pred[256,768]{0,1:T(8,128)(4,1)S(1)} %fusion.92, bf16[256,8,128]{0,2,1:T(8,128)(2,1)S(1)} %bitcast.148, bf16[768,512]{1,0:T(8,128)(2,1)} %get-tuple-element.434, s32[]{:T(128)S(6)} %select_n.77), kind=kOutput, calls=%fused_computation.66.clone.1 | convolution fusion | flops 408945408 | bytes 7217156 | tf_op jit(solution)/shard_map/while/body/eval_jaxpr/sub | solution.py:53
  185.3 3.6 fusion.94
  193.9 1.5 fusion.96
  197.8 5.7 %fusion.93 = (f32[8,256]{1,0:T(8,128)S(1)}, f32[8,256,768]{1,2,0:T(8,128)}) fusion(pred[256,768]{0,1:T(8,128)(4,1)S(1)} %fusion.92, bf16[256,8,128]{0,2,1:T(8,128)(2,1)S(1)} %bitcast.148, bf16[768,512]{1,0:T(8,128)(2,1)} %get-tuple-element.434, s32[]{:T(128)S(6)} %select_n.77), kind=kOutput, calls=%fused_computation.66.clone.1 | convolution fusion | flops 408945408 | bytes 7217156 | tf_op jit(solution)/shard_map/while/body/eval_jaxpr/sub | solution.py:53
  204.2 3.6 fusion.94
  212.9 1.5 fusion.96
  215.5 3.1 slice.24
  219.3 78.9 %reduce-scatter.3.cloned.1.call-done = f32[2,64,512]{2,1,0:T(8,128)} async-done(((f32[2,512,512]{2,1,0:T(8,128)}), f32[2,64,512]{2,1,0:T(8,128)}) %reduce-scatter.3.cloned.1.call-update) | async-done | bytes 262160 | tf_op jit(solution)/shard_map/reduce_scatter | solution.py:95
  298.2 5.3 %broadcast_select_fusion = f32[32,2,64,512]{3,2,1,0:T(8,128)} fusion(f32[2,64,512]{2,1,0:T(8,128)} %reduce-scatter.3.cloned.1.call-done, pred[32]{0:T(512)(128)(4,1)S(1)} %iota_compare_fusion.2), kind=kLoop, calls=%fused_computation.53 | loop fusion | flops 2097152 | bytes 8650784 | tf_op jit(solution)/shard_map/jit(_where)/select_n | solution.py:100
  303.6 2.1 fusion.45
  305.7 128.8 %reduce-scatter.5.cloned.1.call-done = f32[1,2,64,512]{3,2,1,0:T(8,128)} async-done(((f32[32,2,64,512]{3,2,1,0:T(8,128)}), f32[1,2,64,512]{3,2,1,0:T(8,128)}) %reduce-scatter.5.cloned.1.call-update) | async-done | bytes 262160 | tf_op jit(solution)/shard_map/reduce_scatter | solution.py:99
  (104 shorter events, 40.4 us)
Async XLA Ops:
  7.2 78.2 %copy-start.1 = (bf16[1,1,256,4096]{3,2,1,0:T(8,128)(2,1)S(1)}, bf16[1,1,256,4096]{3,2,1,0:T(8,128)(2,1)}, u32[]{:S(2)}) copy-start(bf16[1,1,256,4096]{3,2,1,0:T(8,128)(2,1)} %param.10) | copy-start | bytes 6291460
  7.2 72.5 %all-gather.3.cloned.1.call-start = ((), (), s32[]{:S(2)}) async-start(), calls=%async_computation.2 | async-start | bytes 4325376 | tf_op jit(solution)/shard_map/all_gather | solution.py:20
  7.9 125.5 %all-gather.5.cloned.1.call-start = ((), (), s32[]{:S(2)}) async-start(), calls=%async_computation.3 | async-start | bytes 1179648 | tf_op jit(solution)/shard_map/all_gather | solution.py:22
  81.3 217.0 %reduce-scatter.3.cloned.1.call-start = ((), (), s32[]{:S(2)}) async-start(), calls=%async_computation.4 | async-start | bytes 2359296 | tf_op jit(solution)/shard_map/reduce_scatter | solution.py:95
  85.4 2.5 copy-start.2
  85.4 2.6 copy-start.3
  85.4 2.6 copy-start.5
  147.4 3.6 copy-start
  147.4 5.3 %slice-start = ((s8[6291456]{0:T(1024)(128)(4,1)}), s8[4194304]{0:T(1024)(128)(4,1)S(1)}, s32[]{:S(2)}) async-start(s8[6291456]{0:T(1024)(128)(4,1)} %bitcast.143), calls=%async_computation.6 | async-start | bytes 8388608 | tf_op jit(solution)/shard_map/while
  151.1 1.7 slice-start.1
  166.3 3.6 copy-start
  166.3 5.3 %slice-start = ((s8[6291456]{0:T(1024)(128)(4,1)}), s8[4194304]{0:T(1024)(128)(4,1)S(1)}, s32[]{:S(2)}) async-start(s8[6291456]{0:T(1024)(128)(4,1)} %bitcast.143), calls=%async_computation.6 | async-start | bytes 8388608 | tf_op jit(solution)/shard_map/while
  169.9 1.7 slice-start.1
  185.2 3.6 copy-start
  185.2 5.3 %slice-start = ((s8[6291456]{0:T(1024)(128)(4,1)}), s8[4194304]{0:T(1024)(128)(4,1)S(1)}, s32[]{:S(2)}) async-start(s8[6291456]{0:T(1024)(128)(4,1)} %bitcast.143), calls=%async_computation.6 | async-start | bytes 8388608 | tf_op jit(solution)/shard_map/while
  188.9 1.7 slice-start.1
  204.2 3.6 copy-start
  204.2 5.3 %slice-start = ((s8[6291456]{0:T(1024)(128)(4,1)}), s8[4194304]{0:T(1024)(128)(4,1)S(1)}, s32[]{:S(2)}) async-start(s8[6291456]{0:T(1024)(128)(4,1)} %bitcast.143), calls=%async_computation.6 | async-start | bytes 8388608 | tf_op jit(solution)/shard_map/while
  207.9 1.7 slice-start.1
  215.4 3.1 copy-start.4
  218.6 215.8 %reduce-scatter.5.cloned.1.call-start = ((), (), s32[]{:S(2)}) async-start(), calls=%async_computation.5 | async-start | bytes 8650752 | tf_op jit(solution)/shard_map/reduce_scatter | solution.py:99
Sparse Core Ops, SparseCore 0:
  9.9 69.7 all-gather.2
  82.9 50.4 all-gather.4
  218.7 79.4 reduce-scatter.2
  303.7 130.6 reduce-scatter.4
where the time goes:
time: 442 us; the launch traced here: 441 us
  waiting for transfers between devices  320 us (72%)
  matrix products  44.4 us (10%)
  other arithmetic  31.4 us (7%)
  local copies, waits for them, and re-layouts  28.4 us (6%)
  between operations  15.8 us (4%)
    reduce_scatter x1, waiting for transfers between devices, shards(): lax.psum_scatter(jnp.where(targets == my_parent, token_share[None], 0.0),...  129 us
    reduce_scatter x1, waiting for transfers between devices, shards(): lax.psum_scatter(pair_acc[:, :prefix_len], 'branch', scatter_dimension=1,...  78.9 us
    all_gather x1, waiting for transfers between devices, shards(): gathered = lax.all_gather(prefix_kv, 'prefix', axis=0, tiled=True)  68.5 us
    all_gather x1, waiting for transfers between devices, shards(): whole_prefix = lax.all_gather(picked, 'branch', axis=2, tiled=True)  43.5 us
    sub x4, matrix products, per_head(): shifted = jnp.exp(scores - row_max)  23 us
    convert_element_type x4, other arithmetic, per_head(): weights_low = weights.astype(jnp.bfloat16)  14.3 us
  transfers between devices with their start and end apart: 4, of which 4 were waited for; matrix products, arithmetic and copies ran while one was open for 3% of the time, Pallas kernels for 0%

commit v1 on v0

v1 whole, which is shorter than its diff:
```python
import functools
import jax
import jax.numpy as jnp
from jax import lax
from jax.experimental import pallas as pl
from jax.experimental.pallas import tpu as pltpu
from jax.sharding import Mesh, PartitionSpec as P
QH=32;KVH=4;HD=128;RATIO=8
LOG2E=1.4426950408889634
F32=jnp.float32; BF=jnp.bfloat16

def attn_kernel(len_ref, q_ref, og_ref, vw_ref, vg_ref, bkv_ref, *rest, npieces, plen, unroll):
    pieces=rest[:npieces]
    dq_ref, bg_ref, val_ref = rest[npieces:npieces+3]
    pg = rest[npieces+3:npieces+3+npieces]
    k_s, v_s, kt_s, vt_s, dk_s, dv_s, val_s = rest[npieces+3+npieces:]
    j=pl.program_id(0)
    T=q_ref.shape[0]
    rows=plen//npieces
    S=plen+T
    for i in range(npieces):
        k_s[i*rows:(i+1)*rows,:]=pieces[i][0]
        v_s[i*rows:(i+1)*rows,:]=pieces[i][1]
    k_s[plen:,:]=bkv_ref[0]
    v_s[plen:,:]=bkv_ref[1]
    kt_s[...]=k_s[...].T
    vt_s[...]=v_s[...].T
    dk_s[...]=jnp.zeros_like(dk_s)
    dv_s[...]=jnp.zeros_like(dv_s)
    vg_col=jnp.broadcast_to(vg_ref[...],(8,T)).T[:,:1]
    live=(lax.broadcasted_iota(jnp.int32,(1,T),1)<len_ref[0]).astype(F32)
    key_i=lax.broadcasted_iota(jnp.int32,(T,T),0)
    row_i=lax.broadcasted_iota(jnp.int32,(T,T),1)
    allowed=key_i<=row_i
    scale=HD**-0.5
    @pl.when(j==0)
    def _():
        val_s[...]=jnp.zeros_like(val_s)
    def head(h,_):
        cols=pl.ds(pl.multiple_of(h*HD,HD),HD)
        q=q_ref[:,cols]
        vw=vw_ref[:,cols]
        c=(og_ref[:,cols].astype(F32)+vg_col*vw).astype(BF)
        ct=c.T
        s=lax.dot_general(k_s[...],q,(((1,),(1,)),((),())),preferred_element_type=F32)
        sp=s[:plen]*(scale*LOG2E)
        sb=jnp.where(allowed,s[plen:]*(scale*LOG2E),-1e30)
        m=jnp.maximum(jnp.max(sp,axis=0,keepdims=True),jnp.max(sb,axis=0,keepdims=True))
        pp=jnp.exp2(sp-m); pb=jnp.exp2(sb-m)
        l=jnp.sum(pp,axis=0,keepdims=True)+jnp.sum(pb,axis=0,keepdims=True)
        rl=live/l
        w=jnp.concatenate([pp*rl,pb*rl],axis=0)
        wl=w.astype(BF)
        att=jnp.dot(vt_s[...],wl,preferred_element_type=F32)
        dp=jnp.dot(v_s[...],ct,preferred_element_type=F32)
        delta=jnp.sum(ct.astype(F32)*att,axis=0,keepdims=True)
        val_s[...]+=att*jnp.broadcast_to(vw,(8,HD)).T[:,:1]
        ds=(w*(dp-delta)).astype(BF)
        dq=jnp.dot(kt_s[...],ds,preferred_element_type=F32)*scale
        dq_ref[:,cols]=dq.T.astype(BF)
        dv_s[...]+=jnp.dot(wl,c,preferred_element_type=F32)
        dk_s[...]+=jnp.dot(ds,q,preferred_element_type=F32)
        return 0
    lax.fori_loop(0,RATIO,head,0,unroll=unroll)
    dk=dk_s[...]*scale
    dv=dv_s[...]
    for i in range(npieces):
        pg[i][0]=dk[i*rows:(i+1)*rows].astype(BF)
        pg[i][1]=dv[i*rows:(i+1)*rows].astype(BF)
    bg_ref[0]=dk[plen:].astype(BF)
    bg_ref[1]=dv[plen:].astype(BF)
    @pl.when(j==pl.num_programs(0)-1)
    def _():
        val_ref[...]=jnp.sum(val_s[...],axis=0,keepdims=True)

def attn(lengths,q,og,vw,vg,bkv,pieces,unroll=1):
    T=q.shape[0]; n=len(pieces); rows=pieces[0].shape[1]; plen=rows*n; S=plen+T
    W=RATIO*HD
    col=lambda j:(0,j)
    in_specs=[pl.BlockSpec(memory_space=pltpu.SMEM),
      pl.BlockSpec((T,W),col),pl.BlockSpec((T,W),col),pl.BlockSpec((1,W),col),
      pl.BlockSpec((1,T),lambda j:(0,0)),
      pl.BlockSpec((2,T,HD),lambda j:(0,0,j))]+[pl.BlockSpec((2,rows,HD),lambda j:(0,0,j))]*n
    out_specs=[pl.BlockSpec((T,W),col),pl.BlockSpec((2,T,HD),lambda j:(0,0,j)),pl.BlockSpec((1,T),lambda j:(0,0))]+[pl.BlockSpec((2,rows,HD),lambda j:(0,0,j))]*n
    out_shape=[jax.ShapeDtypeStruct((T,QH*HD),BF),jax.ShapeDtypeStruct((2,T,KVH*HD),BF),jax.ShapeDtypeStruct((1,T),F32)]+[jax.ShapeDtypeStruct((2,rows,KVH*HD),BF)]*n
    return pl.pallas_call(functools.partial(attn_kernel,npieces=n,plen=plen,unroll=unroll),grid=(KVH,),
      in_specs=in_specs,out_specs=out_specs,out_shape=out_shape,
      scratch_shapes=[pltpu.VMEM((S,HD),BF),pltpu.VMEM((S,HD),BF),pltpu.VMEM((HD,S),BF),pltpu.VMEM((HD,S),BF),
        pltpu.VMEM((S,HD),F32),pltpu.VMEM((S,HD),F32),pltpu.VMEM((HD,T),F32)],
      compiler_params=pltpu.CompilerParams(vmem_limit_bytes=48*1024*1024),
    )(lengths,q,og,vw,vg,bkv,*pieces)


Z, YL, CORE, YH, X = 8, 2, 2, 2, 4


def shift(value, axis, step, size):
    return lax.ppermute(value, axis, [(i, (i + step) % size) for i in range(size)])


def gather_z(value):
    got = {0: value}
    for k in (2, -2, 1, -1):
        got[k % Z] = shift(value, "z", k, Z)
    got[4] = shift(got[2], "z", 2, Z)
    got[3] = shift(got[1], "z", 2, Z)
    got[5] = shift(got[7], "z", -2, Z)
    return [got[k] for k in range(Z)]


def pick(index, options):
    out = options[0]
    for k in range(1, len(options)):
        out = jnp.where(index == k, options[k], out)
    return out


def shards(queries, branch_kv, prefix_kv, out_grad, value_weight, value_grad, parents, lengths):
    my_z, my_yl, my_c = lax.axis_index("z"), lax.axis_index("yl"), lax.axis_index("c")
    pair = my_yl * CORE + my_c

    def parent_of(z, other_pair):
        return lax.dynamic_index_in_dim(parents, z * (YL * CORE) + other_pair, 0, keepdims=False)

    ring = gather_z(prefix_kv[0])
    received = []
    for step in range(YL * CORE):
        wanted = parent_of(my_z, (pair + step) % (YL * CORE))
        sent = pick((my_z - wanted // (YL * CORE)) % Z, ring)
        received.append(shift(sent, ("yl", "c"), step, YL * CORE) if step else sent)
    mine = parent_of(my_z, pair)
    picked = pick((pair - mine % (YL * CORE)) % (YL * CORE), received)

    row = [picked] + [shift(picked, "x", k, X) for k in range(1, X)]
    pieces = row + [shift(piece, "yh", 1, YH) for piece in row]

    query_grad, branch_grad, values, *piece_grads = attn(
        lengths[0], queries[0, 0], out_grad[0, 0], value_weight[None], value_grad[0], branch_kv[0, 0], pieces)

    back = []
    for index, piece in enumerate(piece_grads):
        jy, k = divmod(index, X)
        perm = [(i, ((i // X - jy) % YH) * X + (i % X - k) % X) for i in range(YH * X)]
        back.append(lax.ppermute(piece, ("yh", "x"), perm) if index else piece)
    share = sum(piece.astype(F32) for piece in back).astype(BF)

    ring = gather_z(share)
    owners = [parent_of((my_z - k) % Z, pair) for k in range(Z)]
    received = []
    for step in range(YL * CORE):
        target = (pair + step) % (YL * CORE)
        slot = sum(
            jnp.where(owners[k] == my_z * (YL * CORE) + target, ring[k].astype(F32), 0.0) for k in range(Z))
        received.append(
            shift(slot.astype(BF), ("yl", "c"), step, YL * CORE).astype(F32) if step else slot)
    prefix_grad = sum(received)
    return values[None], query_grad[None, None], branch_grad[None, None], prefix_grad[None]


def solution(mesh):
    fine = Mesh(mesh.devices.reshape(Z, YL, CORE, YH, X), ("z", "yl", "c", "yh", "x"))
    prefix, branch = ("z", "yl", "c"), ("yh", "x")
    in_specs = (
        P(prefix, branch, None, None),
        P(prefix, branch, None, None, None),
        P(prefix, None, branch, None),
        P(prefix, branch, None, None),
        P(),
        P(prefix, branch, None),
        P(),
        P(prefix, branch),
    )
    out_specs = (
        P(prefix, branch, None),
        P(prefix, branch, None, None),
        P(prefix, branch, None, None, None),
        P(prefix, None, branch, None),
    )
    return jax.shard_map(shards, mesh=fine, in_specs=in_specs, out_specs=out_specs, check_vma=False)
```

time: 442 us -> 173 us (0.39)
  waiting for transfers between devices: 320 us -> 25 us
  starting transfers between devices: 0.16 us -> 57.2 us
  Pallas kernels: 0 us -> 45.3 us
  matrix products: 44.4 us -> 0 us
  local copies, waits for them, and re-layouts: 28.4 us -> 2.5 us
  other arithmetic: 31.4 us -> 7.78 us
  between operations: 15.8 us -> 33.7 us
    reduce_scatter x2 -> x0, waiting for transfers between devices: 208 us -> none  [the longest x1 129 us: shards(): lax.psum_scatter(jnp.where(targets == my_parent, token_share[None], 0.0),...]
    all_gather x2 -> x0, waiting for transfers between devices: 112 us -> none  [the longest x1 68.5 us: shards(): gathered = lax.all_gather(prefix_kv, 'prefix', axis=0, tiled=True)]
    ppermute x0 -> x34, starting transfers between devices: none -> 57.2 us  [the longest x27 43.5 us: shift(): lax.ppermute(value, axis, [(i, (i + step) % size) for i in range(size)])]
    pallas_call x0 -> x1, Pallas kernels: none -> 45.3 us  [attn(): pl.pallas_call(functools.partial(attn_kernel, npieces=n, plen=plen, unrol...]
    ppermute x0 -> x34, waiting for transfers between devices: none -> 25 us  [the longest x27 18.1 us: shift(): lax.ppermute(value, axis, [(i, (i + step) % size) for i in range(size)])]
    sub x4 -> x0, matrix products: 23 us -> none  [per_head(): shifted = jnp.exp(scores - row_max)]
    dot_general x20 -> x0, matrix products: 21.5 us -> none  [the longest x4 6.13 us: per_head(): jnp.einsum('rts,sd->trd', score_low, key_part, preferred_element_type=jnp...]
    convert_element_type x5 -> x4, other arithmetic: 16.3 us -> 0.77 us  [the longest x3 0.63 us: shards(): slot.astype(BF)]
  transfers between devices with their start and end apart: 4 -> 34, of which waited for: 4 -> 10; matrix products, arithmetic and copies ran while one was open for 3% -> 3% of each run, Pallas kernels for 0% -> 0%
where the time goes in v1:
time: 173 us; the launch traced here: 171 us
  starting transfers between devices  57.2 us (33%)
  Pallas kernels  45.3 us (26%)
  between operations  33.7 us (19%)
  waiting for transfers between devices  25 us (14%)
  other arithmetic  7.78 us (4%)
  local copies, waits for them, and re-layouts  2.5 us (1%)
    pallas_call x1, Pallas kernels, attn(): pl.pallas_call(functools.partial(attn_kernel, npieces=n, plen=plen, unrol...  45.3 us
    ppermute x27, starting transfers between devices, shift(): lax.ppermute(value, axis, [(i, (i + step) % size) for i in range(size)])  43.5 us
    ppermute x27, waiting for transfers between devices, shift(): lax.ppermute(value, axis, [(i, (i + step) % size) for i in range(size)])  18.1 us
    ppermute x7, starting transfers between devices, shards(): back.append(lax.ppermute(piece, ('yh', 'x'), perm) if index else piece)  13.7 us
    ppermute x7, waiting for transfers between devices, shards(): back.append(lax.ppermute(piece, ('yh', 'x'), perm) if index else piece)  6.86 us
    select_n x4, other arithmetic, pick(): out = jnp.where(index == k, options[k], out)  6.05 us
  transfers between devices with their start and end apart: 34, of which 10 were waited for; matrix products, arithmetic and copies ran while one was open for 3% of the time, Pallas kernels for 0%

profile of v1, /device:TPU:4, one launch (start us, length us, event | category | flops | bytes accessed | tf_op | source)
XLA Modules:
  0.0 171.5 jit_solution(13749875368963669273)
XLA Ops:
  0.6 5.9 %collective-permute-start = (bf16[2,64,512]{2,1,0:T(8,128)(2,1)}, bf16[2,64,512]{2,1,0:T(8,128)(2,1)S(1)}, u32[]{:S(2)}, u32[]{:S(2)}) collective-permute-start(bf16[2,64,512]{2,1,0:T(8,128)(2,1)} %bitcast.35), channel_id=1, source_target_pairs={{0,224},{32,0},{64,32},{96,64},{128,96},{160,128},{192,160},{224,1... | collective-permute-start | bytes 393224 | tf_op jit(solution)/shard_map/ppermute | solution.py:98
  6.6 4.1 %collective-permute-start.1 = (bf16[2,64,512]{2,1,0:T(8,128)(2,1)}, bf16[2,64,512]{2,1,0:T(8,128)(2,1)S(1)}, u32[]{:S(2)}, u32[]{:S(2)}) collective-permute-start(bf16[2,64,512]{2,1,0:T(8,128)(2,1)} %bitcast.38), channel_id=1, source_target_pairs={{0,192},{32,224},{64,0},{96,32},{128,64},{160,96},{192,128},{224,1... | collective-permute-start | bytes 393224 | tf_op jit(solution)/shard_map/ppermute | solution.py:98
  10.7 1.8 %collective-permute-start.2 = (bf16[2,64,512]{2,1,0:T(8,128)(2,1)S(1)}, bf16[2,64,512]{2,1,0:T(8,128)(2,1)S(1)}, u32[]{:S(2)}, u32[]{:S(2)}) collective-permute-start(bf16[2,64,512]{2,1,0:T(8,128)(2,1)S(1)} %collective-permute-done), channel_id=1, source_target_pairs={{0,192},{32,224},{64,0},{96,32},{128,64},{160,96},{192,128},{224,1... | collective-permute-start | bytes 393224 | tf_op jit(solution)/shard_map/ppermute | solution.py:98
  12.5 5.0 %collective-permute-done.3 = bf16[2,64,512]{2,1,0:T(8,128)(2,1)S(1)} collective-permute-done((bf16[2,64,512]{2,1,0:T(8,128)(2,1)}, bf16[2,64,512]{2,1,0:T(8,128)(2,1)S(1)}, u32[]{:S(2)}, u32[]{:S(2)}) %collective-permute-start.3) | collective-permute-done | bytes 131104 | tf_op jit(solution)/shard_map/ppermute | solution.py:98
  17.9 1.8 %fusion.35 = (s32[1]{0:T(128)}, s32[1]{0:T(128)}, s32[1]{0:T(128)}, s32[1]{0:T(128)}, s32[1]{0:T(128)}, /*index=5*/s32[1]{0:T(128)}, s32[1]{0:T(128)}, s32[1]{0:...) fusion(s32[32]{0:T(128)} %param.14, s32[]{:T(128)S(6)} %select_n.600, ...), kind=kLoop, calls=%fused_computation.72 | loop fusion | bytes 156 | tf_op jit(solution)/shard_map/jit(dynamic_index_in_dim)/dynamic_slice | solution.py:123
  27.7 2.5 %collective-permute-done.6 = bf16[2,64,512]{2,1,0:T(8,128)(2,1)S(1)} collective-permute-done((bf16[2,64,512]{2,1,0:T(8,128)(2,1)S(1)}, bf16[2,64,512]{2,1,0:T(8,128)(2,1)S(1)}, u32[]{:S(2)}, u32[]{:S(2)}) %collective-permute-start.6) | collective-permute-done | bytes 131104 | tf_op jit(solution)/shard_map/ppermute | solution.py:98
  32.6 1.8 %select_select_fusion.2 = bf16[2,64,512]{2,1,0:T(8,128)(2,1)} fusion(bf16[2,64,512]{2,1,0:T(8,128)(2,1)S(1)} %collective-permute-done, bf16[2,64,512]{2,1,0:T(8,128)(2,1)S(1)} %collective-permute-done.1, bf16[2,64,512]{2,1,0:T(8,128)(2,1)S(1)} %collective-permute-done.2, bf16[2,64,512]{2,1,0:T(8,128)(2,1)} %copy-done.5, bf16[2,64,512]{2,1,0:T(8,128)(2,1)} %copy-done.6, ...), kind=kLoop, calls=%fused_computation.70 | loop fusion | flops 458752 | bytes 1179655 | tf_op jit(solution)/shard_map/jit(_where)/select_n | solution.py:114
  47.7 2.9 %collective-permute-start.13 = (bf16[2,64,512]{2,1,0:T(8,128)(2,1)S(1)}, bf16[2,64,512]{2,1,0:T(8,128)(2,1)S(1)}, u32[]{:S(2)}, u32[]{:S(2)}) collective-permute-start(bf16[2,64,512]{2,1,0:T(8,128)(2,1)S(1)} %select_select_fusion.rest_0_), channel_id=1, source_target_pairs={{0,4},{4,0},{1,5},{5,1},{2,6},{6,2},{3,7},{7,3},{8,12},{12,8},{9,1... | collective-permute-start | bytes 393224 | tf_op jit(solution)/shard_map/ppermute | solution.py:98
  50.7 2.9 %collective-permute-start.14 = (bf16[2,64,512]{2,1,0:T(8,128)(2,1)S(1)}, bf16[2,64,512]{2,1,0:T(8,128)(2,1)S(1)}, u32[]{:S(2)}, u32[]{:S(2)}) collective-permute-start(bf16[2,64,512]{2,1,0:T(8,128)(2,1)S(1)} %collective-permute-done.10.rest_1_), channel_id=1, source_target_pairs={{0,4},{4,0},{1,5},{5,1},{2,6},{6,2},{3,7},{7,3},{8,12},{12,8},{9,1... | collective-permute-start | bytes 393224 | tf_op jit(solution)/shard_map/ppermute | solution.py:98
  55.1 2.0 %collective-permute-start.16 = (bf16[2,64,512]{2,1,0:T(8,128)(2,1)S(1)}, bf16[2,64,512]{2,1,0:T(8,128)(2,1)S(1)}, u32[]{:S(2)}, u32[]{:S(2)}) collective-permute-start(bf16[2,64,512]{2,1,0:T(8,128)(2,1)S(1)} %collective-permute-done.12.rest_3_), channel_id=1, source_target_pairs={{0,4},{4,0},{1,5},{5,1},{2,6},{6,2},{3,7},{7,3},{8,12},{12,8},{9,1... | collective-permute-start | bytes 393224 | tf_op jit(solution)/shard_map/ppermute | solution.py:98
  57.9 2.4 %collective-permute-done.15.rest_6_ = bf16[2,64,512]{2,1,0:T(8,128)(2,1)S(1)} collective-permute-done((bf16[2,64,512]{2,1,0:T(8,128)(2,1)S(1)}, bf16[2,64,512]{2,1,0:T(8,128)(2,1)S(1)}, u32[]{:S(2)}, u32[]{:S(2)}) %collective-permute-start.15) | collective-permute-done | bytes 131104 | tf_op jit(solution)/shard_map/ppermute | solution.py:98
  61.7 45.3 %shard_map.111 = (bf16[256,4096]{1,0:T(8,128)(2,1)}, bf16[2,256,512]{2,1,0:T(8,128)(2,1)}, f32[1,256]{1,0:T(1,128)}, bf16[2,64,512]{2,1,0:T(8,128)(2,1)S(1)}, bf...) custom-call(s32[1]{0:T(128)} %bitcast.29.len_ref, ...), custom_call_target="tpu_custom_call" | custom-call | tf_op jit(solution)/shard_map/pallas_call | solution.py:86
  107.1 2.2 %collective-permute-start.17 = (bf16[2,64,512]{2,1,0:T(8,128)(2,1)S(1)}, bf16[2,64,512]{2,1,0:T(8,128)(2,1)S(1)}, u32[]{:S(2)}, u32[]{:S(2)}) collective-permute-start(bf16[2,64,512]{2,1,0:T(8,128)(2,1)S(1)} %get-tuple-element.19), channel_id=1, source_target_pairs={{0,3},{1,0},{2,1},{3,2},{4,7},{5,4},{6,5},{7,6},{8,11},{9,8},{10,9... | collective-permute-start | bytes 393224 | tf_op jit(solution)/shard_map/ppermute | solution.py:144
  110.4 2.3 %collective-permute-start.19 = (bf16[2,64,512]{2,1,0:T(8,128)(2,1)S(1)}, bf16[2,64,512]{2,1,0:T(8,128)(2,1)S(1)}, u32[]{:S(2)}, u32[]{:S(2)}) collective-permute-start(bf16[2,64,512]{2,1,0:T(8,128)(2,1)S(1)} %get-tuple-element.21), channel_id=1, source_target_pairs={{0,1},{1,2},{2,3},{3,0},{4,5},{5,6},{6,7},{7,4},{8,9},{9,10},{10,1... | collective-permute-start | bytes 393224 | tf_op jit(solution)/shard_map/ppermute | solution.py:144
  112.7 1.9 %collective-permute-start.20 = (bf16[2,64,512]{2,1,0:T(8,128)(2,1)S(1)}, bf16[2,64,512]{2,1,0:T(8,128)(2,1)S(1)}, u32[]{:S(2)}, u32[]{:S(2)}) collective-permute-start(bf16[2,64,512]{2,1,0:T(8,128)(2,1)S(1)} %get-tuple-element.22), channel_id=1, source_target_pairs={{0,4},{1,5},{2,6},{3,7},{4,0},{5,1},{6,2},{7,3},{8,12},{9,13},{10,... | collective-permute-start | bytes 393224 | tf_op jit(solution)/shard_map/ppermute | solution.py:144
  115.4 4.9 %collective-permute-start.22 = (bf16[2,64,512]{2,1,0:T(8,128)(2,1)S(1)}, bf16[2,64,512]{2,1,0:T(8,128)(2,1)S(1)}, u32[]{:S(2)}, u32[]{:S(2)}) collective-permute-start(bf16[2,64,512]{2,1,0:T(8,128)(2,1)S(1)} %get-tuple-element.24), channel_id=1, source_target_pairs={{0,6},{1,7},{2,4},{3,5},{4,2},{5,3},{6,0},{7,1},{8,14},{9,15},{10,... | collective-permute-start | bytes 393224 | tf_op jit(solution)/shard_map/ppermute | solution.py:144
  120.8 4.1 %collective-permute-done.20 = bf16[2,64,512]{2,1,0:T(8,128)(2,1)S(1)} collective-permute-done((bf16[2,64,512]{2,1,0:T(8,128)(2,1)S(1)}, bf16[2,64,512]{2,1,0:T(8,128)(2,1)S(1)}, u32[]{:S(2)}, u32[]{:S(2)}) %collective-permute-start.20) | collective-permute-done | bytes 131104 | tf_op jit(solution)/shard_map/ppermute | solution.py:144
  124.9 2.7 %collective-permute-done.23 = bf16[2,64,512]{2,1,0:T(8,128)(2,1)S(1)} collective-permute-done((bf16[2,64,512]{2,1,0:T(8,128)(2,1)S(1)}, bf16[2,64,512]{2,1,0:T(8,128)(2,1)S(1)}, u32[]{:S(2)}, u32[]{:S(2)}) %collective-permute-start.23) | collective-permute-done | bytes 131104 | tf_op jit(solution)/shard_map/ppermute | solution.py:144
  127.8 2.2 %collective-permute-start.24 = (bf16[2,64,512]{2,1,0:T(8,128)(2,1)S(1)}, bf16[2,64,512]{2,1,0:T(8,128)(2,1)S(1)}, u32[]{:S(2)}, u32[]{:S(2)}) collective-permute-start(bf16[2,64,512]{2,1,0:T(8,128)(2,1)S(1)} %add_convert_fusion), channel_id=1, source_target_pairs={{0,32},{32,64},{64,96},{96,128},{128,160},{160,192},{192,224},{224... | collective-permute-start | bytes 393224 | tf_op jit(solution)/shard_map/ppermute | solution.py:98
  131.6 2.2 %collective-permute-start.28 = (bf16[2,64,512]{2,1,0:T(8,128)(2,1)S(1)}, bf16[2,64,512]{2,1,0:T(8,128)(2,1)S(1)}, u32[]{:S(2)}, u32[]{:S(2)}) collective-permute-start(bf16[2,64,512]{2,1,0:T(8,128)(2,1)S(1)} %add_convert_fusion), channel_id=1, source_target_pairs={{0,224},{32,0},{64,32},{96,64},{128,96},{160,128},{192,160},{224,1... | collective-permute-start | bytes 393224 | tf_op jit(solution)/shard_map/ppermute | solution.py:98
  134.1 1.7 %collective-permute-done.24 = bf16[2,64,512]{2,1,0:T(8,128)(2,1)S(1)} collective-permute-done((bf16[2,64,512]{2,1,0:T(8,128)(2,1)S(1)}, bf16[2,64,512]{2,1,0:T(8,128)(2,1)S(1)}, u32[]{:S(2)}, u32[]{:S(2)}) %collective-permute-start.24) | collective-permute-done | bytes 131104 | tf_op jit(solution)/shard_map/ppermute | solution.py:98
  135.8 2.6 %collective-permute-start.26 = (bf16[2,64,512]{2,1,0:T(8,128)(2,1)S(1)}, bf16[2,64,512]{2,1,0:T(8,128)(2,1)S(1)}, u32[]{:S(2)}, u32[]{:S(2)}) collective-permute-start(bf16[2,64,512]{2,1,0:T(8,128)(2,1)S(1)} %collective-permute-done.24), channel_id=1, source_target_pairs={{0,64},{32,96},{64,128},{96,160},{128,192},{160,224},{192,0},{224,... | collective-permute-start | bytes 393224 | tf_op jit(solution)/shard_map/ppermute | solution.py:98
  138.4 4.7 %collective-permute-done.25 = bf16[2,64,512]{2,1,0:T(8,128)(2,1)S(1)} collective-permute-done((bf16[2,64,512]{2,1,0:T(8,128)(2,1)S(1)}, bf16[2,64,512]{2,1,0:T(8,128)(2,1)S(1)}, u32[]{:S(2)}, u32[]{:S(2)}) %collective-permute-start.25) | collective-permute-done | bytes 131104 | tf_op jit(solution)/shard_map/ppermute | solution.py:98
  143.2 4.1 %collective-permute-start.29 = (bf16[2,64,512]{2,1,0:T(8,128)(2,1)S(1)}, bf16[2,64,512]{2,1,0:T(8,128)(2,1)S(1)}, u32[]{:S(2)}, u32[]{:S(2)}) collective-permute-start(bf16[2,64,512]{2,1,0:T(8,128)(2,1)S(1)} %collective-permute-done.28), channel_id=1, source_target_pairs={{0,192},{32,224},{64,0},{96,32},{128,64},{160,96},{192,128},{224,1... | collective-permute-start | bytes 393224 | tf_op jit(solution)/shard_map/ppermute | solution.py:98
  (69 shorter events, 23.4 us)
Async XLA Ops:
  0.6 10.1 %collective-permute-start = (bf16[2,64,512]{2,1,0:T(8,128)(2,1)}, bf16[2,64,512]{2,1,0:T(8,128)(2,1)S(1)}, u32[]{:S(2)}, u32[]{:S(2)}) collective-permute-start(bf16[2,64,512]{2,1,0:T(8,128)(2,1)} %bitcast.35), channel_id=1, source_target_pairs={{0,224},{32,0},{64,32},{96,64},{128,96},{160,128},{192,160},{224,1... | collective-permute-start | bytes 393224 | tf_op jit(solution)/shard_map/ppermute | solution.py:98
  6.6 10.9 %collective-permute-start.3 = (bf16[2,64,512]{2,1,0:T(8,128)(2,1)}, bf16[2,64,512]{2,1,0:T(8,128)(2,1)S(1)}, u32[]{:S(2)}, u32[]{:S(2)}) collective-permute-start(bf16[2,64,512]{2,1,0:T(8,128)(2,1)} %bitcast.36), channel_id=1, source_target_pairs={{0,64},{32,96},{64,128},{96,160},{128,192},{160,224},{192,0},{224,... | collective-permute-start | bytes 393224 | tf_op jit(solution)/shard_map/ppermute | solution.py:98
  6.6 10.9 %collective-permute-start.5 = (bf16[2,64,512]{2,1,0:T(8,128)(2,1)}, bf16[2,64,512]{2,1,0:T(8,128)(2,1)S(1)}, u32[]{:S(2)}, u32[]{:S(2)}) collective-permute-start(bf16[2,64,512]{2,1,0:T(8,128)(2,1)} %bitcast.37), channel_id=1, source_target_pairs={{0,32},{32,64},{64,96},{96,128},{128,160},{160,192},{192,224},{224... | collective-permute-start | bytes 393224 | tf_op jit(solution)/shard_map/ppermute | solution.py:98
  6.6 21.1 %collective-permute-start.1 = (bf16[2,64,512]{2,1,0:T(8,128)(2,1)}, bf16[2,64,512]{2,1,0:T(8,128)(2,1)S(1)}, u32[]{:S(2)}, u32[]{:S(2)}) collective-permute-start(bf16[2,64,512]{2,1,0:T(8,128)(2,1)} %bitcast.38), channel_id=1, source_target_pairs={{0,192},{32,224},{64,0},{96,32},{128,64},{160,96},{192,128},{224,1... | collective-permute-start | bytes 393224 | tf_op jit(solution)/shard_map/ppermute | solution.py:98
  10.7 16.9 %collective-permute-start.2 = (bf16[2,64,512]{2,1,0:T(8,128)(2,1)S(1)}, bf16[2,64,512]{2,1,0:T(8,128)(2,1)S(1)}, u32[]{:S(2)}, u32[]{:S(2)}) collective-permute-start(bf16[2,64,512]{2,1,0:T(8,128)(2,1)S(1)} %collective-permute-done), channel_id=1, source_target_pairs={{0,192},{32,224},{64,0},{96,32},{128,64},{160,96},{192,128},{224,1... | collective-permute-start | bytes 393224 | tf_op jit(solution)/shard_map/ppermute | solution.py:98
  17.5 10.1 %collective-permute-start.4 = (bf16[2,64,512]{2,1,0:T(8,128)(2,1)S(1)}, bf16[2,64,512]{2,1,0:T(8,128)(2,1)S(1)}, u32[]{:S(2)}, u32[]{:S(2)}) collective-permute-start(bf16[2,64,512]{2,1,0:T(8,128)(2,1)S(1)} %collective-permute-done.3), channel_id=1, source_target_pairs={{0,64},{32,96},{64,128},{96,160},{128,192},{160,224},{192,0},{224,... | collective-permute-start | bytes 393224 | tf_op jit(solution)/shard_map/ppermute | solution.py:98
  17.5 12.7 %collective-permute-start.6 = (bf16[2,64,512]{2,1,0:T(8,128)(2,1)S(1)}, bf16[2,64,512]{2,1,0:T(8,128)(2,1)S(1)}, u32[]{:S(2)}, u32[]{:S(2)}) collective-permute-start(bf16[2,64,512]{2,1,0:T(8,128)(2,1)S(1)} %collective-permute-done.5), channel_id=1, source_target_pairs={{0,64},{32,96},{64,128},{96,160},{128,192},{160,224},{192,0},{224,... | collective-permute-start | bytes 393224 | tf_op jit(solution)/shard_map/ppermute | solution.py:98
  32.5 10.9 %collective-permute-start.9 = (bf16[2,64,512]{2,1,0:T(8,128)(2,1)}, bf16[2,64,512]{2,1,0:T(8,128)(2,1)}, u32[]{:S(2)}, u32[]{:S(2)}) collective-permute-start(bf16[2,64,512]{2,1,0:T(8,128)(2,1)} %select_select_fusion.1), channel_id=1, source_target_pairs={{0,8},{8,16},{16,24},{24,0},{1,9},{9,17},{17,25},{25,1},{2,10},{10... | collective-permute-start | bytes 393224 | tf_op jit(solution)/shard_map/ppermute | solution.py:98
  34.4 9.0 %collective-permute-start.8 = (bf16[2,64,512]{2,1,0:T(8,128)(2,1)}, bf16[2,64,512]{2,1,0:T(8,128)(2,1)}, u32[]{:S(2)}, u32[]{:S(2)}) collective-permute-start(bf16[2,64,512]{2,1,0:T(8,128)(2,1)} %select_select_fusion.2), channel_id=1, source_target_pairs={{0,16},{8,24},{16,0},{24,8},{1,17},{9,25},{17,1},{25,9},{2,18},{10... | collective-permute-start | bytes 393224 | tf_op jit(solution)/shard_map/ppermute | solution.py:98
  46.5 8.6 %collective-permute-start.12 = (bf16[2,64,512]{2,1,0:T(8,128)(2,1)S(1)}, bf16[2,64,512]{2,1,0:T(8,128)(2,1)S(1)}, u32[]{:S(2)}, u32[]{:S(2)}) collective-permute-start(bf16[2,64,512]{2,1,0:T(8,128)(2,1)S(1)} %select_select_fusion.rest_0_), channel_id=1, source_target_pairs={{0,3},{1,0},{2,1},{3,2},{4,7},{5,4},{6,5},{7,6},{8,11},{9,8},{10,9... | collective-permute-start | bytes 393224 | tf_op jit(solution)/shard_map/ppermute | solution.py:98
  47.7 10.1 %collective-permute-start.13 = (bf16[2,64,512]{2,1,0:T(8,128)(2,1)S(1)}, bf16[2,64,512]{2,1,0:T(8,128)(2,1)S(1)}, u32[]{:S(2)}, u32[]{:S(2)}) collective-permute-start(bf16[2,64,512]{2,1,0:T(8,128)(2,1)S(1)} %select_select_fusion.rest_0_), channel_id=1, source_target_pairs={{0,4},{4,0},{1,5},{5,1},{2,6},{6,2},{3,7},{7,3},{8,12},{12,8},{9,1... | collective-permute-start | bytes 393224 | tf_op jit(solution)/shard_map/ppermute | solution.py:98
  107.1 8.3 %collective-permute-start.17 = (bf16[2,64,512]{2,1,0:T(8,128)(2,1)S(1)}, bf16[2,64,512]{2,1,0:T(8,128)(2,1)S(1)}, u32[]{:S(2)}, u32[]{:S(2)}) collective-permute-start(bf16[2,64,512]{2,1,0:T(8,128)(2,1)S(1)} %get-tuple-element.19), channel_id=1, source_target_pairs={{0,3},{1,0},{2,1},{3,2},{4,7},{5,4},{6,5},{7,6},{8,11},{9,8},{10,9... | collective-permute-start | bytes 393224 | tf_op jit(solution)/shard_map/ppermute | solution.py:144
  109.2 11.0 %collective-permute-start.18 = (bf16[2,64,512]{2,1,0:T(8,128)(2,1)S(1)}, bf16[2,64,512]{2,1,0:T(8,128)(2,1)S(1)}, u32[]{:S(2)}, u32[]{:S(2)}) collective-permute-start(bf16[2,64,512]{2,1,0:T(8,128)(2,1)S(1)} %get-tuple-element.20), channel_id=1, source_target_pairs={{0,2},{1,3},{2,0},{3,1},{4,6},{5,7},{6,4},{7,5},{8,10},{9,11},{10,... | collective-permute-start | bytes 393224 | tf_op jit(solution)/shard_map/ppermute | solution.py:144
  110.4 10.4 %collective-permute-start.19 = (bf16[2,64,512]{2,1,0:T(8,128)(2,1)S(1)}, bf16[2,64,512]{2,1,0:T(8,128)(2,1)S(1)}, u32[]{:S(2)}, u32[]{:S(2)}) collective-permute-start(bf16[2,64,512]{2,1,0:T(8,128)(2,1)S(1)} %get-tuple-element.21), channel_id=1, source_target_pairs={{0,1},{1,2},{2,3},{3,0},{4,5},{5,6},{6,7},{7,4},{8,9},{9,10},{10,1... | collective-permute-start | bytes 393224 | tf_op jit(solution)/shard_map/ppermute | solution.py:144
  112.7 12.2 %collective-permute-start.20 = (bf16[2,64,512]{2,1,0:T(8,128)(2,1)S(1)}, bf16[2,64,512]{2,1,0:T(8,128)(2,1)S(1)}, u32[]{:S(2)}, u32[]{:S(2)}) collective-permute-start(bf16[2,64,512]{2,1,0:T(8,128)(2,1)S(1)} %get-tuple-element.22), channel_id=1, source_target_pairs={{0,4},{1,5},{2,6},{3,7},{4,0},{5,1},{6,2},{7,3},{8,12},{9,13},{10,... | collective-permute-start | bytes 393224 | tf_op jit(solution)/shard_map/ppermute | solution.py:144
  114.6 10.3 %collective-permute-start.21 = (bf16[2,64,512]{2,1,0:T(8,128)(2,1)S(1)}, bf16[2,64,512]{2,1,0:T(8,128)(2,1)S(1)}, u32[]{:S(2)}, u32[]{:S(2)}) collective-permute-start(bf16[2,64,512]{2,1,0:T(8,128)(2,1)S(1)} %get-tuple-element.23), channel_id=1, source_target_pairs={{0,7},{1,4},{2,5},{3,6},{4,3},{5,0},{6,1},{7,2},{8,15},{9,12},{10,... | collective-permute-start | bytes 393224 | tf_op jit(solution)/shard_map/ppermute | solution.py:144
  115.4 9.5 %collective-permute-start.22 = (bf16[2,64,512]{2,1,0:T(8,128)(2,1)S(1)}, bf16[2,64,512]{2,1,0:T(8,128)(2,1)S(1)}, u32[]{:S(2)}, u32[]{:S(2)}) collective-permute-start(bf16[2,64,512]{2,1,0:T(8,128)(2,1)S(1)} %get-tuple-element.24), channel_id=1, source_target_pairs={{0,6},{1,7},{2,4},{3,5},{4,2},{5,3},{6,0},{7,1},{8,14},{9,15},{10,... | collective-permute-start | bytes 393224 | tf_op jit(solution)/shard_map/ppermute | solution.py:144
  129.9 13.2 %collective-permute-start.25 = (bf16[2,64,512]{2,1,0:T(8,128)(2,1)S(1)}, bf16[2,64,512]{2,1,0:T(8,128)(2,1)S(1)}, u32[]{:S(2)}, u32[]{:S(2)}) collective-permute-start(bf16[2,64,512]{2,1,0:T(8,128)(2,1)S(1)} %add_convert_fusion), channel_id=1, source_target_pairs={{0,64},{32,96},{64,128},{96,160},{128,192},{160,224},{192,0},{224,... | collective-permute-start | bytes 393224 | tf_op jit(solution)/shard_map/ppermute | solution.py:98
  131.6 11.6 %collective-permute-start.28 = (bf16[2,64,512]{2,1,0:T(8,128)(2,1)S(1)}, bf16[2,64,512]{2,1,0:T(8,128)(2,1)S(1)}, u32[]{:S(2)}, u32[]{:S(2)}) collective-permute-start(bf16[2,64,512]{2,1,0:T(8,128)(2,1)S(1)} %add_convert_fusion), channel_id=1, source_target_pairs={{0,224},{32,0},{64,32},{96,64},{128,96},{160,128},{192,160},{224,1... | collective-permute-start | bytes 393224 | tf_op jit(solution)/shard_map/ppermute | solution.py:98
  133.8 28.4 %collective-permute-start.30 = (bf16[2,64,512]{2,1,0:T(8,128)(2,1)S(1)}, bf16[2,64,512]{2,1,0:T(8,128)(2,1)S(1)}, u32[]{:S(2)}, u32[]{:S(2)}) collective-permute-start(bf16[2,64,512]{2,1,0:T(8,128)(2,1)S(1)} %add_convert_fusion), channel_id=1, source_target_pairs={{0,192},{32,224},{64,0},{96,32},{128,64},{160,96},{192,128},{224,1... | collective-permute-start | bytes 393224 | tf_op jit(solution)/shard_map/ppermute | solution.py:98
  135.8 26.4 %collective-permute-start.26 = (bf16[2,64,512]{2,1,0:T(8,128)(2,1)S(1)}, bf16[2,64,512]{2,1,0:T(8,128)(2,1)S(1)}, u32[]{:S(2)}, u32[]{:S(2)}) collective-permute-start(bf16[2,64,512]{2,1,0:T(8,128)(2,1)S(1)} %collective-permute-done.24), channel_id=1, source_target_pairs={{0,64},{32,96},{64,128},{96,160},{128,192},{160,224},{192,0},{224,... | collective-permute-start | bytes 393224 | tf_op jit(solution)/shard_map/ppermute | solution.py:98
  143.2 19.0 %collective-permute-start.27 = (bf16[2,64,512]{2,1,0:T(8,128)(2,1)S(1)}, bf16[2,64,512]{2,1,0:T(8,128)(2,1)S(1)}, u32[]{:S(2)}, u32[]{:S(2)}) collective-permute-start(bf16[2,64,512]{2,1,0:T(8,128)(2,1)S(1)} %collective-permute-done.25), channel_id=1, source_target_pairs={{0,64},{32,96},{64,128},{96,160},{128,192},{160,224},{192,0},{224,... | collective-permute-start | bytes 393224 | tf_op jit(solution)/shard_map/ppermute | solution.py:98
  143.2 19.0 %collective-permute-start.29 = (bf16[2,64,512]{2,1,0:T(8,128)(2,1)S(1)}, bf16[2,64,512]{2,1,0:T(8,128)(2,1)S(1)}, u32[]{:S(2)}, u32[]{:S(2)}) collective-permute-start(bf16[2,64,512]{2,1,0:T(8,128)(2,1)S(1)} %collective-permute-done.28), channel_id=1, source_target_pairs={{0,192},{32,224},{64,0},{96,32},{128,64},{160,96},{192,128},{224,1... | collective-permute-start | bytes 393224 | tf_op jit(solution)/shard_map/ppermute | solution.py:98
  162.4 8.1 %collective-permute-start.31 = (bf16[2,64,512]{2,1,0:T(8,128)(2,1)S(1)}, bf16[2,64,512]{2,1,0:T(8,128)(2,1)S(1)}, u32[]{:S(2)}, u32[]{:S(2)}) collective-permute-start(bf16[2,64,512]{2,1,0:T(8,128)(2,1)S(1)} %fusion.18), channel_id=1, source_target_pairs={{0,8},{8,16},{16,24},{24,0},{1,9},{9,17},{17,25},{25,1},{2,10},{10... | collective-permute-start | bytes 393224 | tf_op jit(solution)/shard_map/ppermute | solution.py:98
  (17 other events, 225.7 us)
